TPU v7x, 256 devices: a whole 4x4x8 slice. The times are simulated.
256 devices in a mesh: batch: 8 (over x, core), branch: 32 (over z, y).
Axes of the slice: x: 4, y: 4, z: 8, core: 2. Of those that a mesh axis runs over, the one named last changes fastest.
Arguments:
- queries: bfloat16 [256, 128, 16, 128], P(('batch', 'branch')), parts along dimension 0, may hold values from -6 to 6
- response_keys: bfloat16 [256, 128, 4, 128], P(('batch', 'branch')), parts along dimension 0, may hold values from -6 to 6
- response_values: bfloat16 [256, 128, 4, 128], P(('batch', 'branch')), parts along dimension 0, may hold values from -6 to 6
- prompt_keys: bfloat16 [16384, 4, 128], P(('batch', 'branch')), parts along dimension 0, may hold values from -6 to 6
- prompt_value_rows: bfloat16 [16384, 4, 128], P(('batch', 'branch')), parts along dimension 0, may hold values from -6 to 6
- lengths: int32 [256], P(('batch', 'branch')), parts along dimension 0, may hold values from 16 to 128, as said below
- grad_out: bfloat16 [256, 128, 16, 128], P(('batch', 'branch')), parts along dimension 0, may hold values from -6 to 6
Outputs:
- attended: bfloat16 [256, 128, 16, 128], P(('batch', 'branch')), parts along dimension 0
- grad_query: bfloat16 [256, 128, 16, 128], P(('batch', 'branch')), parts along dimension 0
- grad_resp_keys: bfloat16 [256, 128, 4, 128], P(('batch', 'branch')), parts along dimension 0
- grad_resp_values: bfloat16 [256, 128, 4, 128], P(('batch', 'branch')), parts along dimension 0
- grad_prompt_keys: bfloat16 [16384, 4, 128], P(('batch', 'branch')), parts along dimension 0
- grad_prompt_values: bfloat16 [16384, 4, 128], P(('batch', 'branch')), parts along dimension 0
There are 8 independent parts, one for each index of `batch`. A program takes and returns all parts, laid end to end along the dimension named above; each array names one. Nothing has to cross between parts.
Inputs may be any that keep to these rules, and one draw needn't show every extreme that they name: `lengths`: some response of every prompt has all 128 slots live.
All inputs are finite; a program needn't handle non-finite values.
Results may differ from a plain program's by a relative error of at most 0.034.
Values may be sent and summed in bfloat16 or wider, within the bound.
No kernel may reach another device: no remote copies, remote signals or barrier semaphores. Data moves between devices by JAX's collectives and lax.ppermute only.
A program may use at most 192 MiB of HBM per device.

v0:
```python
import jax
import jax.numpy as jnp
from jax import lax
from jax.sharding import PartitionSpec as P

masked_score = -1e30


def local_attention(
    queries, response_keys, response_values, whole_keys, whole_values, lengths, grad_out
):
    resp_count, seq_len, num_heads, head_dim = queries.shape
    kv_heads = whole_keys.shape[1]
    group_size = num_heads // kv_heads
    score_scale = head_dim ** (-0.5)
    grouped = queries.reshape(resp_count, seq_len, kv_heads, group_size, head_dim)
    row_ids = jnp.arange(seq_len)
    causal = row_ids[None, :] <= row_ids[:, None]
    live_rows = row_ids[None, :] < lengths[:, None]
    live_wide = live_rows[:, :, None, None, None]
    grad_grouped = grad_out.reshape(resp_count, seq_len, kv_heads, group_size, head_dim)
    masked = jnp.where(live_wide, grad_grouped, jnp.zeros_like(grad_grouped))
    prompt_scores = (
        jnp.einsum("rtkgd,skd->rkgts", grouped, whole_keys, preferred_element_type=jnp.float32)
        * score_scale
    )
    own_scores = (
        jnp.einsum("rtkgd,rskd->rkgts", grouped, response_keys, preferred_element_type=jnp.float32)
        * score_scale
    )
    own_scores = jnp.where(causal, own_scores, masked_score)
    top_score = jnp.maximum(
        jnp.max(prompt_scores, axis=-1, keepdims=True), jnp.max(own_scores, axis=-1, keepdims=True)
    )
    total = jnp.sum(jnp.exp(prompt_scores - top_score), axis=-1, keepdims=True) + jnp.sum(
        jnp.exp(own_scores - top_score), axis=-1, keepdims=True
    )
    log_total = top_score + jnp.log(total)
    prompt_weights = jnp.exp(prompt_scores - log_total)
    own_weights = jnp.exp(own_scores - log_total)
    prompt_low = prompt_weights.astype(jnp.bfloat16)
    own_low = own_weights.astype(jnp.bfloat16)
    attended = jnp.einsum(
        "rkgts,skd->rtkgd", prompt_low, whole_values, preferred_element_type=jnp.float32
    )
    attended = attended + jnp.einsum(
        "rkgts,rskd->rtkgd", own_low, response_values, preferred_element_type=jnp.float32
    )
    attended = jnp.where(live_wide, attended, 0.0).astype(jnp.bfloat16)
    row_delta = jnp.sum(masked.astype(jnp.float32) * attended.astype(jnp.float32), axis=-1)
    row_delta = jnp.transpose(row_delta, (0, 2, 3, 1))
    prompt_dw = jnp.einsum(
        "rtkgd,skd->rkgts", masked, whole_values, preferred_element_type=jnp.float32
    )
    own_dw = jnp.einsum(
        "rtkgd,rskd->rkgts", masked, response_values, preferred_element_type=jnp.float32
    )
    prompt_ds = (prompt_weights * (prompt_dw - row_delta[..., None])).astype(jnp.bfloat16)
    own_ds = (own_weights * (own_dw - row_delta[..., None])).astype(jnp.bfloat16)
    grad_query = jnp.einsum(
        "rkgts,skd->rtkgd", prompt_ds, whole_keys, preferred_element_type=jnp.float32
    )
    grad_query = grad_query + jnp.einsum(
        "rkgts,rskd->rtkgd", own_ds, response_keys, preferred_element_type=jnp.float32
    )
    grad_query = (grad_query * score_scale).astype(jnp.bfloat16)
    grad_rk = (
        jnp.einsum("rkgts,rtkgd->rskd", own_ds, grouped, preferred_element_type=jnp.float32)
        * score_scale
    ).astype(jnp.bfloat16)
    grad_rv = jnp.einsum(
        "rkgts,rtkgd->rskd", own_low, masked, preferred_element_type=jnp.float32
    ).astype(jnp.bfloat16)
    return (
        attended.reshape(resp_count, seq_len, num_heads, head_dim),
        grad_query.reshape(resp_count, seq_len, num_heads, head_dim),
        grad_rk,
        grad_rv,
        prompt_ds,
        prompt_low,
        grouped,
        masked,
        log_total[..., 0],
        row_delta,
    )


def take_rows(prompt_dk, prompt_dv):
    return jnp.stack([prompt_dk, prompt_dv], axis=1)


def on_device(
    queries, response_keys, response_values, prompt_keys, prompt_value_rows, lengths, grad_out
):
    whole_keys, whole_values = (
        lax.all_gather(prompt_keys, "branch", axis=0, tiled=True),
        lax.all_gather(prompt_value_rows, "branch", axis=0, tiled=True),
    )
    (
        attended,
        grad_query,
        grad_rk,
        grad_rv,
        prompt_ds,
        prompt_low,
        grouped,
        masked,
        log_total,
        row_delta,
    ) = local_attention(
        queries, response_keys, response_values, whole_keys, whole_values, lengths, grad_out
    )
    score_scale = queries.shape[-1] ** (-0.5)
    local_dk = (
        jnp.einsum("rkgts,rtkgd->skd", prompt_ds, grouped, preferred_element_type=jnp.float32)
        * score_scale
    )
    local_dv = jnp.einsum(
        "rkgts,rtkgd->skd", prompt_low, masked, preferred_element_type=jnp.float32
    )
    shares = lax.psum_scatter(
        take_rows(local_dk, local_dv).astype(jnp.bfloat16),
        "branch",
        scatter_dimension=0,
        tiled=True,
    ).astype(jnp.float32)
    prompt_dk = shares[:, 0]
    prompt_dv = shares[:, 1]
    return (
        attended,
        grad_query,
        grad_rk,
        grad_rv,
        prompt_dk.astype(jnp.bfloat16),
        prompt_dv.astype(jnp.bfloat16),
    )


def solution(mesh):
    return jax.shard_map(
        on_device,
        mesh=mesh,
        in_specs=(
            P(("batch", "branch"), None, None, None),
            P(("batch", "branch"), None, None, None),
            P(("batch", "branch"), None, None, None),
            P(("batch", "branch"), None, None),
            P(("batch", "branch"), None, None),
            P(("batch", "branch")),
            P(("batch", "branch"), None, None, None),
        ),
        out_specs=(
            P(("batch", "branch"), None, None, None),
            P(("batch", "branch"), None, None, None),
            P(("batch", "branch"), None, None, None),
            P(("batch", "branch"), None, None, None),
            P(("batch", "branch"), None, None),
            P(("batch", "branch"), None, None),
        ),
        check_vma=False,
    )
```

profile of v0, /device:TPU:2, one launch (start us, length us, event | category | flops | bytes accessed | tf_op | source)
XLA Modules:
  0.0 424.4 jit_solution(5410509129297976514)
XLA Ops:
  7.2 1.5 copy.13
  8.8 0.0 all-gather.5.cloned.1.call-start
  8.8 1.5 copy.17
  10.3 0.0 reduce-scatter.2.cloned.1.call-start
  10.4 2.2 copy.24
  13.3 1.5 copy.21
  14.8 1.2 fusion.65
  16.0 76.1 %all-gather.3.cloned.1.call-done = bf16[2048,4,128]{2,0,1:T(8,128)(2,1)} async-done(((bf16[64,4,128]{2,0,1:T(8,128)(2,1)}), bf16[2048,4,128]{2,0,1:T(8,128)(2,1)}) %all-gather.3.cloned.1.call-update) | async-done | bytes 2097168 | tf_op jit(solution)/shard_map/all_gather | solution.py:96
  92.2 9.7 %bitcast_reduce_fusion = (f32[4,4,128]{2,1,0:T(4,128)S(1)}, f32[4,2048,128,4]{2,1,3,0:T(8,128)}) fusion(bf16[128,4,4,128]{3,2,1,0:T(4,128)(2,1)S(1)} %bitcast.201, bf16[2048,4,128]{2,0,1:T(8,128)(2,1)} %all-gather.3.cloned.1.call-done), kind=kOutput, calls=%fused_computation.5 | convolution fusion | flops 1082128384 | bytes 19406848 | tf_op jit(solution)/shard_map/rtkgd,skd->rkgts/dot_general | solution.py:24
  101.8 0.2 exponential_reduce_fusion
  102.0 8.6 %fusion.3 = f32[4,4,128]{2,1,0:T(4,128)S(1)} fusion(f32[4,2048,128,4]{2,1,3,0:T(8,128)} %get-tuple-element.15, f32[4,4,128]{2,1,0:T(4,128)S(1)} %max.11), kind=kLoop, calls=%fused_computation.7 | loop fusion | flops 12580864 | bytes 16793600 | tf_op jit(solution)/shard_map/reduce_sum | solution.py:35
  110.6 10.0 %fusion.9 = bf16[2048,1,4,128]{3,0,2,1:T(8,128)(2,1)} fusion(f32[4,2048,128,4]{2,1,3,0:T(8,128)} %get-tuple-element.15, f32[4,4,128]{2,1,0:T(4,128)S(1)} %bitcast.213, bf16[128,4,4,128]{0,3,2,1:T(8,128)(2,1)S(1)} %copy.21, pred[128]{0:T(512)(128)(4,1)S(1)} %iota_compare_fusion.1), kind=kOutput, calls=%fused_computation.16 | convolution fusion | flops 1087635456 | bytes 19406976 | tf_op jit(solution)/shard_map/rkgts,rtkgd->skd/dot_general | solution.py:118
  120.6 49.9 %all-gather.5.cloned.1.call-done = bf16[2048,4,128]{2,0,1:T(8,128)(2,1)} async-done(((bf16[64,4,128]{2,0,1:T(8,128)(2,1)}), bf16[2048,4,128]{2,0,1:T(8,128)(2,1)}) %all-gather.5.cloned.1.call-update) | async-done | bytes 2097168 | tf_op jit(solution)/shard_map/all_gather | solution.py:97
  170.5 8.1 %fusion.18 = f32[1,128,4,4,128]{1,4,3,2,0:T(8,128)S(1)} fusion(bf16[2048,4,128]{2,0,1:T(8,128)(2,1)} %all-gather.5.cloned.1.call-done, f32[4,2048,128,4]{2,1,3,0:T(8,128)} %get-tuple-element.15, f32[4,4,128]{2,1,0:T(4,128)S(1)} %bitcast.214), kind=kOutput, calls=%fused_computation.25 | convolution fusion | flops 1086324736 | bytes 19931136 | tf_op jit(solution)/shard_map/rkgts,skd->rtkgd/dot_general | solution.py:43
  178.6 2.3 multiply_reduce_fusion
  180.9 8.5 %fusion.7 = bf16[4,4,128,2048]{2,3,1,0:T(8,128)(2,1)S(1)} fusion(f32[4,2048,128,4]{2,1,3,0:T(8,128)} %get-tuple-element.15, f32[4,4,128]{2,1,0:T(4,128)S(1)} %bitcast.220, f32[4,4,128]{2,1,0:T(4,128)S(1)} %bitcast.216, bf16[2048,4,128]{2,0,1:T(8,128)(2,1)} %all-gather.5.cloned.1.call-done, bf16[128,4,4,128]{0,3,2,1:T(8,128)(2,1)S(1)} %copy.21, ...), kind=kOutput, calls=%fused_computation.11 | convolution fusion | flops 1094975488 | bytes 27803776 | tf_op jit(solution)/shard_map/rtkgd,skd->rkgts/dot_general | solution.py:52
  189.4 3.2 copy-done.1
  192.6 2.4 fusion.10
  195.0 2.3 pad_maximum_fusion
  197.3 1.2 copy.36
  198.5 0.3 fusion.35
  198.9 6.9 %fusion.21 = f32[1,128,4,4,128]{4,1,3,2,0:T(8,128)S(1)} fusion(bf16[4,4,128,2048]{2,3,1,0:T(8,128)(2,1)} %copy-done.1, bf16[2048,4,128]{2,0,1:T(8,128)(2,1)} %all-gather.3.cloned.1.call-done), kind=kOutput, calls=%fused_computation.26 | convolution fusion | flops 1073741824 | bytes 11534336 | tf_op jit(solution)/shard_map/rkgts,skd->rtkgd/dot_general | solution.py:60
  205.8 0.4 fusion.33
  206.2 1.1 copy.37
  207.3 0.3 fusion.42
  207.6 0.8 copy.38
  208.3 0.3 fusion.41
  208.7 0.8 copy.39
  209.5 206.2 %reduce-scatter.2.cloned.1.call-done = bf16[64,2,4,128]{3,0,2,1:T(8,128)(2,1)} async-done(((bf16[2048,2,4,128]{3,0,2,1:T(8,128)(2,1)}), bf16[64,2,4,128]{3,0,2,1:T(8,128)(2,1)}) %reduce-scatter.2.cloned.1.call-update) | async-done | bytes 131088 | tf_op jit(solution)/shard_map/reduce_scatter | solution.py:121
  415.7 0.9 slice_bitcast_fusion
  416.5 0.7 copy.40
  417.2 0.7 copy.41
  (19 shorter events, 0.2 us)
Async XLA Ops:
  7.2 7.6 %copy-start = (bf16[1,128,16,128]{3,2,1,0:T(8,128)(2,1)S(1)}, bf16[1,128,16,128]{3,2,1,0:T(8,128)(2,1)}, u32[]{:S(2)}) copy-start(bf16[1,128,16,128]{3,2,1,0:T(8,128)(2,1)} %param.7) | copy-start | bytes 1572868
  7.2 85.0 %all-gather.3.cloned.1.call-start = ((), (), s32[]{:S(2)}) async-start(), calls=%async_computation.1 | async-start | bytes 2162688 | tf_op jit(solution)/shard_map/all_gather | solution.py:96
  8.8 161.7 %all-gather.5.cloned.1.call-start = ((), (), s32[]{:S(2)}) async-start(), calls=%async_computation.2 | async-start | bytes 2162688 | tf_op jit(solution)/shard_map/all_gather | solution.py:97
  10.3 405.3 %reduce-scatter.2.cloned.1.call-start = ((), (), s32[]{:S(2)}) async-start(), calls=%async_computation.3 | async-start | bytes 4325376 | tf_op jit(solution)/shard_map/reduce_scatter | solution.py:121
  120.6 58.0 %copy-start.4 = (bf16[1,128,4,128]{3,2,1,0:T(4,128)(2,1)S(1)}, bf16[1,128,4,128]{3,2,1,0:T(4,128)(2,1)}, u32[]{:S(2)}) copy-start(bf16[1,128,4,128]{3,2,1,0:T(4,128)(2,1)} %param.9) | copy-start | bytes 393220
  189.4 3.2 copy-start.1
  192.6 2.4 copy-start.2
  195.0 2.4 copy-start.3
  198.8 6.9 %copy-start.5 = (bf16[1,128,4,128]{3,2,1,0:T(4,128)(2,1)S(1)}, bf16[1,128,4,128]{3,2,1,0:T(4,128)(2,1)}, u32[]{:S(2)}) copy-start(bf16[1,128,4,128]{3,2,1,0:T(4,128)(2,1)} %param.8) | copy-start | bytes 393220
Sparse Core Ops, SparseCore 0:
  11.2 80.9 all-gather.2
  95.3 75.0 all-gather.4
  197.4 218.1 reduce-scatter.1
where the time goes:
time: 425 us; the launch traced here: 424 us
  waiting for transfers between devices  332 us (78%)
  matrix products  50.3 us (12%)
  local copies, waits for them, and re-layouts  16.1 us (4%)
  between operations  14.6 us (3%)
  other arithmetic  11.1 us (3%)
    reduce_scatter x1, waiting for transfers between devices, on_device(): lax.psum_scatter(take_rows(local_dk, local_dv).astype(jnp.bfloat16), 'bra...  206 us
    all_gather x1, waiting for transfers between devices, on_device(): lax.all_gather(prompt_keys, 'branch', axis=0, tiled=True)  76.1 us
    all_gather x1, waiting for transfers between devices, on_device(): lax.all_gather(prompt_value_rows, 'branch', axis=0, tiled=True)  49.9 us
    unnamed x21, local copies, waits for them, and re-layouts  13.7 us
    dot_general x1, matrix products, on_device(): jnp.einsum('rkgts,rtkgd->skd', prompt_low, masked, preferred_element_type...  9.96 us
    dot_general x1, matrix products, local_attention(): jnp.einsum('rtkgd,skd->rkgts', grouped, whole_keys, preferred_element_typ...  9.66 us
    reduce_sum x1, other arithmetic, local_attention(): jnp.sum(jnp.exp(prompt_scores - top_score), axis=-1, keepdims=True)  8.57 us
  transfers between devices with their start and end apart: 3, of which 3 were waited for; matrix products, arithmetic and copies ran while one was open for 11% of the time, Pallas kernels for 0%

commit v1 on v0

--- a/solution.py
+++ b/solution.py
@@ -94,7 +94,12 @@
 ):
     whole_keys, whole_values = (
         lax.all_gather(prompt_keys, "branch", axis=0, tiled=True),
-        lax.all_gather(prompt_value_rows, "branch", axis=0, tiled=True),
+        jnp.concatenate(
+            lax.all_to_all(
+                jnp.stack([prompt_value_rows] * lax.axis_size("branch")), "branch", 0, 0
+            ),
+            axis=0,
+        ),
     )
     (
         attended,

time: 425 us -> 383 us (0.901)
  waiting for transfers between devices: 332 us -> 277 us
  starting transfers between devices: 0.12 us -> 11.7 us
    all_gather x1 -> x0, waiting for transfers between devices: 49.9 us -> none  [on_device(): lax.all_gather(prompt_value_rows, 'branch', axis=0, tiled=True)]
    all_to_all x0 -> x1, starting transfers between devices: none -> 11.6 us  [on_device(): lax.all_to_all(jnp.stack([prompt_value_rows] * lax.axis_size('branch')),...]
    all_gather x1, waiting for transfers between devices: 76.1 us -> 70.8 us  [on_device(): lax.all_gather(prompt_keys, 'branch', axis=0, tiled=True)]
    unnamed x21 -> x29, local copies, waits for them, and re-layouts: 13.7 us -> 13.1 us
  transfers between devices with their start and end apart: 3 -> 3, of which waited for: 3 -> 2; matrix products, arithmetic and copies ran while one was open for 11% -> 10% of each run, Pallas kernels for 0% -> 0%
where the time goes in v1:
time: 383 us; the launch traced here: 382 us
  waiting for transfers between devices  277 us (72%)
  matrix products  48.5 us (13%)
  local copies, waits for them, and re-layouts  19.1 us (5%)
  between operations  14.9 us (4%)
  starting transfers between devices  11.7 us (3%)
  other arithmetic  11.1 us (3%)
    reduce_scatter x1, waiting for transfers between devices, on_device(): lax.psum_scatter(take_rows(local_dk, local_dv).astype(jnp.bfloat16), 'bra...  206 us
    all_gather x1, waiting for transfers between devices, on_device(): lax.all_gather(prompt_keys, 'branch', axis=0, tiled=True)  70.8 us
    unnamed x29, local copies, waits for them, and re-layouts  13.1 us
    all_to_all x1, starting transfers between devices, on_device(): lax.all_to_all(jnp.stack([prompt_value_rows] * lax.axis_size('branch')),...  11.6 us
    dot_general x1, matrix products, local_attention(): jnp.einsum('rkgts,skd->rtkgd', prompt_low, whole_values, preferred_elemen...  9.77 us
    dot_general x1, matrix products, local_attention(): jnp.einsum('rtkgd,skd->rkgts', grouped, whole_keys, preferred_element_typ...  9.67 us
    dot_general x1, matrix products, on_device(): jnp.einsum('rkgts,rtkgd->skd', prompt_low, masked, preferred_element_type...  9 us
    reduce_sum x1, other arithmetic, local_attention(): jnp.sum(jnp.exp(prompt_scores - top_score), axis=-1, keepdims=True)  8.54 us
  transfers between devices with their start and end apart: 3, of which 2 were waited for; matrix products, arithmetic and copies ran while one was open for 10% of the time, Pallas kernels for 0%

profile of v1, /device:TPU:2, one launch (start us, length us, event | category | flops | bytes accessed | tf_op | source)
XLA Modules:
  0.0 382.4 jit_solution(14626327553298380470)
XLA Ops:
  7.2 1.5 copy.73
  8.8 0.9 copy.77
  9.7 1.8 stack.11
  11.5 11.6 %all-to-all-start = ((bf16[32,64,4,128]{3,1,2,0:T(8,128)(2,1)}), bf16[32,64,4,128]{3,1,2,0:T(8,128)(2,1)}, u32[]{:S(2)}, u32[]{:S(2)}) async-start(bf16[32,64,4,128]{3,1,2,0:T(8,128)(2,1)} %stack.11), calls=%async_computation | async-start | bytes 4194304 | tf_op jit(solution)/shard_map/all_to_all | solution.py:98
  23.2 2.2 copy.86
  26.1 1.5 copy.83
  27.6 0.3 fusion.59
  27.9 70.8 %all-gather.2.cloned.1.call-done = bf16[2048,4,128]{2,0,1:T(8,128)(2,1)} async-done(((bf16[64,4,128]{2,0,1:T(8,128)(2,1)}), bf16[2048,4,128]{2,0,1:T(8,128)(2,1)}) %all-gather.2.cloned.1.call-update) | async-done | bytes 2097168 | tf_op jit(solution)/shard_map/all_gather | solution.py:96
  98.7 9.7 %bitcast_reduce_fusion = (f32[4,4,128]{2,1,0:T(4,128)S(1)}, f32[4,2048,128,4]{2,1,3,0:T(8,128)}) fusion(bf16[128,4,4,128]{3,2,1,0:T(4,128)(2,1)S(1)} %bitcast.202, bf16[2048,4,128]{2,0,1:T(8,128)(2,1)} %all-gather.2.cloned.1.call-done), kind=kOutput, calls=%fused_computation.5 | convolution fusion | flops 1082128384 | bytes 19406848 | tf_op jit(solution)/shard_map/rtkgd,skd->rkgts/dot_general | solution.py:24
  108.4 0.2 exponential_reduce_fusion
  108.6 8.5 %fusion.3 = f32[4,4,128]{2,1,0:T(4,128)S(1)} fusion(f32[4,2048,128,4]{2,1,3,0:T(8,128)} %get-tuple-element.27, f32[4,4,128]{2,1,0:T(4,128)S(1)} %max.11), kind=kLoop, calls=%fused_computation.7 | loop fusion | flops 12580864 | bytes 16793600 | tf_op jit(solution)/shard_map/reduce_sum | solution.py:35
  117.2 1.8 copy.78
  118.9 9.8 %convolution_bitcast_fusion.3 = f32[1,128,4,4,128]{1,4,3,2,0:T(8,128)} fusion(bf16[2048,4,128,1]{2,0,3,1:T(8,128)(2,1)S(1)} %bitcast.206, f32[4,2048,128,4]{2,1,3,0:T(8,128)} %get-tuple-element.27, f32[4,4,128]{2,1,0:T(4,128)S(1)} %bitcast.216), kind=kOutput, calls=%fused_computation.26 | convolution fusion | flops 1086324736 | bytes 19931136 | tf_op jit(solution)/shard_map/rkgts,skd->rtkgd/dot_general | solution.py:43
  128.7 9.0 %fusion.9 = bf16[2048,1,4,128]{3,0,2,1:T(8,128)(2,1)S(1)} fusion(f32[4,2048,128,4]{2,1,3,0:T(8,128)} %get-tuple-element.27, f32[4,4,128]{2,1,0:T(4,128)S(1)} %bitcast.217, bf16[128,4,4,128]{0,3,2,1:T(8,128)(2,1)S(1)} %copy.83, pred[128]{0:T(512)(128)(4,1)S(1)} %iota_compare_fusion.1), kind=kOutput, calls=%fused_computation.16 | convolution fusion | flops 1087635456 | bytes 19406976 | tf_op jit(solution)/shard_map/rkgts,rtkgd->skd/dot_general | solution.py:123
  137.8 1.2 multiply_reduce_fusion
  139.0 7.9 %fusion.7 = bf16[4,4,128,2048]{2,3,1,0:T(8,128)(2,1)S(1)} fusion(f32[4,2048,128,4]{2,1,3,0:T(8,128)} %get-tuple-element.27, f32[4,4,128]{2,1,0:T(4,128)S(1)} %bitcast.223, f32[4,4,128]{2,1,0:T(4,128)S(1)} %bitcast.219, bf16[2048,4,128,1]{2,0,3,1:T(8,128)(2,1)S(1)} %bitcast.207, bf16[128,4,4,128]{0,3,2,1:T(8,128)(2,1)S(1)} %copy.83, ...), kind=kOutput, calls=%fused_computation.11 | convolution fusion | flops 1094975488 | bytes 27803776 | tf_op jit(solution)/shard_map/rtkgd,skd->rkgts/dot_general | solution.py:52
  146.9 3.2 copy-done.1
  150.1 2.3 fusion.10
  152.5 2.3 pad_maximum_fusion
  154.9 1.2 copy.98
  156.1 0.3 fusion.29
  156.4 6.9 %fusion.15 = f32[1,128,4,4,128]{4,1,3,2,0:T(8,128)S(1)} fusion(bf16[4,4,128,2048]{2,3,1,0:T(8,128)(2,1)} %copy-done.1, bf16[2048,4,128]{2,0,1:T(8,128)(2,1)} %all-gather.2.cloned.1.call-done), kind=kOutput, calls=%fused_computation.22 | convolution fusion | flops 1073741824 | bytes 11534336 | tf_op jit(solution)/shard_map/rkgts,skd->rtkgd/dot_general | solution.py:60
  163.3 0.4 fusion.27
  163.7 1.1 copy.99
  164.8 0.3 fusion.36
  165.1 0.8 copy.100
  165.9 0.3 fusion.35
  166.2 0.8 copy.101
  167.0 206.4 %reduce-scatter.2.cloned.1.call-done = bf16[64,2,4,128]{3,0,2,1:T(8,128)(2,1)} async-done(((bf16[2048,2,4,128]{3,0,2,1:T(8,128)(2,1)}), bf16[64,2,4,128]{3,0,2,1:T(8,128)(2,1)}) %reduce-scatter.2.cloned.1.call-update) | async-done | bytes 131088 | tf_op jit(solution)/shard_map/reduce_scatter | solution.py:126
  373.4 0.9 slice_bitcast_fusion
  374.2 0.7 copy.102
  374.9 0.7 copy.103
  (28 shorter events, 0.2 us)
Async XLA Ops:
  7.2 20.4 %copy-start = (bf16[1,128,16,128]{3,2,1,0:T(8,128)(2,1)S(1)}, bf16[1,128,16,128]{3,2,1,0:T(8,128)(2,1)}, u32[]{:S(2)}) copy-start(bf16[1,128,16,128]{3,2,1,0:T(8,128)(2,1)} %param.7) | copy-start | bytes 1572868
  7.2 20.4 %copy-start.9 = (bf16[1,128,4,128]{3,2,1,0:T(4,128)(2,1)S(1)}, bf16[1,128,4,128]{3,2,1,0:T(4,128)(2,1)}, u32[]{:S(2)}) copy-start(bf16[1,128,4,128]{3,2,1,0:T(4,128)(2,1)} %param.8) | copy-start | bytes 393220
  7.2 91.6 %all-gather.2.cloned.1.call-start = ((), (), s32[]{:S(2)}) async-start(), calls=%async_computation.2 | async-start | bytes 2162688 | tf_op jit(solution)/shard_map/all_gather | solution.py:96
  11.5 105.7 %all-to-all-start = ((bf16[32,64,4,128]{3,1,2,0:T(8,128)(2,1)}), bf16[32,64,4,128]{3,1,2,0:T(8,128)(2,1)}, u32[]{:S(2)}, u32[]{:S(2)}) async-start(bf16[32,64,4,128]{3,1,2,0:T(8,128)(2,1)} %stack.11), calls=%async_computation | async-start | bytes 4194304 | tf_op jit(solution)/shard_map/all_to_all | solution.py:98
  23.1 350.2 %reduce-scatter.2.cloned.1.call-start = ((), (), s32[]{:S(2)}) async-start(), calls=%async_computation.3 | async-start | bytes 4325376 | tf_op jit(solution)/shard_map/reduce_scatter | solution.py:126
  27.9 80.5 %copy-start.2 = (f32[1,4,4,128,128]{3,4,2,1,0:T(8,128)}, f32[1,4,4,128,128]{3,4,2,1,0:T(8,128)S(1)}, u32[]{:S(2)}) copy-start(f32[1,4,4,128,128]{3,4,2,1,0:T(8,128)S(1)} %get-tuple-element.29) | copy-start | bytes 3145732
  128.7 9.0 %copy-start.3 = (f32[1,4,4,128,128]{3,4,2,1,0:T(8,128)S(1)}, f32[1,4,4,128,128]{3,4,2,1,0:T(8,128)}, u32[]{:S(2)}) copy-start(f32[1,4,4,128,128]{3,4,2,1,0:T(8,128)} %copy-done.2) | copy-start | bytes 3145732
  128.7 9.0 %copy-start.5 = (f32[1,128,4,4,128]{1,4,3,2,0:T(8,128)S(1)}, f32[1,128,4,4,128]{1,4,3,2,0:T(8,128)}, u32[]{:S(2)}) copy-start(f32[1,128,4,4,128]{1,4,3,2,0:T(8,128)} %convolution_bitcast_fusion.3) | copy-start | bytes 3145732
  128.7 9.0 %copy-start.6 = (bf16[1,128,16,128]{1,3,2,0:T(8,128)(2,1)S(1)}, bf16[1,128,16,128]{1,3,2,0:T(8,128)(2,1)}, u32[]{:S(2)}) copy-start(bf16[1,128,16,128]{1,3,2,0:T(8,128)(2,1)} %copy.86) | copy-start | bytes 1572868
  128.7 9.0 %copy-start.8 = (bf16[1,128,4,128]{3,2,1,0:T(4,128)(2,1)S(1)}, bf16[1,128,4,128]{3,2,1,0:T(4,128)(2,1)}, u32[]{:S(2)}) copy-start(bf16[1,128,4,128]{3,2,1,0:T(4,128)(2,1)} %param.9) | copy-start | bytes 393220
  146.9 3.2 copy-start.1
  152.5 2.4 copy-start.7
  152.5 3.6 copy-start.4
Sparse Core Ops, SparseCore 0:
  11.2 87.5 all-gather.1
  155.0 218.3 reduce-scatter.1
